TPU v7x, 1024 devices: a whole 4x8x16 slice. The times are simulated.
1024 devices in a mesh: row: 16 (over z_hi, y), col: 64 (over x, z_lo, core).
Axes of the slice: x: 4, y: 8, z: 16 (z_hi: 2, z_lo: 8; z = z_hi * 8 + z_lo), core: 2. Of those that a mesh axis runs over, the one named last changes fastest.
Arguments:
- a_blocks: float32 [16, 192, 384, 128], P('row', 'col'), may hold values from -0.5 to 0.5
- a_rowid: int32 [16, 192, 3], P('row', 'col'), may hold values from 0 to 3
- a_count: int32 [16, 192], P('row', 'col'), may hold values from 0 to 3
- b_blocks: float32 [16, 192, 128, 384], P('row', 'col'), may hold values from -6 to 6
- b_colid: int32 [16, 192, 3], P('row', 'col'), may hold values from 0 to 5
- b_count: int32 [16, 192], P('row', 'col'), may hold values from 0 to 3
- dest_row: int32 [16, 1536, 1], P('row', 'col'), may hold values from 0 to 15; in each aligned block of 24 rows (0 to 23, 24 to 47, ..., all dimensions but the last counted through in order) at most 2 rows name the same one
Outputs:
- owned_blocks: float32 [16, 2048, 128, 128], P('row', 'col')
Inputs may be any that keep to these rules, and one draw needn't show every extreme that they name: `dest_row`: among the 24 product blocks of one device, at most 2 name any one owner row, and some device's blocks name one owner row exactly 2 times.
All inputs are finite; a program needn't handle non-finite values.
Results may differ from a plain program's by a relative error of at most 0.0003.
Values sent between devices are 32-bit elements; how exact they have to be, the bound alone decides.
A program may use at most 64 MiB of HBM per device.

v0:
```python
import jax
import jax.numpy as jnp
from jax import lax
from jax.sharding import PartitionSpec as P

RB = 4
CB = 6


def passed_along(value, axis, by):
    peers = lax.axis_size(axis)
    return lax.ppermute(value, axis, [(i, (i + by) % peers) for i in range(peers)])


def local_terms(a_state, b_state):
    a_panel = a_state[0][0]
    a_rows = a_state[1][0]
    a_used = a_state[2][0]
    b_panel = b_state[0][0]
    b_cols = b_state[1][0]
    b_used = b_state[2][0]
    block_edge = a_panel.shape[-1]
    slot_count = a_rows.shape[-1]
    inner_count = a_rows.shape[0]
    slot_iota = jnp.arange(slot_count, dtype=jnp.int32)
    a_live = slot_iota[None, :] < a_used[:, None]
    b_live = slot_iota[None, :] < b_used[:, None]
    row_hot = (
        (a_rows[:, :, None] == jnp.arange(RB, dtype=jnp.int32)[None, None, :]) & a_live[:, :, None]
    ).astype(jnp.float32)
    col_hot = (
        (b_cols[:, :, None] == jnp.arange(CB, dtype=jnp.int32)[None, None, :]) & b_live[:, :, None]
    ).astype(jnp.float32)
    slot_prod = jnp.einsum("kxb,kby->kxy", a_panel, b_panel, precision=lax.Precision.HIGHEST)
    slot_prod = slot_prod.reshape(inner_count, slot_count, block_edge, slot_count, block_edge)
    pair_hot = jnp.einsum("kti,kuj->ktiuj", row_hot, col_hot)
    return jnp.einsum("ktiuj,ktpuq->ipjq", pair_hot, slot_prod, precision=lax.Precision.HIGHEST)


def per_device(a_blocks, a_rowid, a_count, b_blocks, b_colid, b_count, dest_row):
    block_edge = a_blocks.shape[-1]
    a_state = (a_blocks, a_rowid, a_count)
    b_state = (b_blocks, b_colid, b_count)
    running = local_terms(a_state, b_state)
    moving_a = a_state
    moving_b = b_state
    for stride in range(2):
        moving_a = passed_along((moving_a[0], moving_a[1], moving_a[2]), "col", -1)
        moving_b = passed_along((moving_b[0], moving_b[1], moving_b[2]), "row", -1)
        running = running + local_terms(moving_a, moving_b)
    block_total = RB * CB
    products = running.transpose(0, 2, 1, 3).reshape(block_total, block_edge, block_edge)
    grid_rows = lax.axis_size("row")
    capacity = max(2, block_total // grid_rows + 1)
    targets = dest_row[0, :, 0]
    block_iota = jnp.arange(block_total, dtype=jnp.int32)
    earlier = (targets[:, None] == targets[None, :]) & (block_iota[None, :] < block_iota[:, None])
    slot_rank = jnp.sum(earlier.astype(jnp.int32), axis=1)
    picked = (targets[None, None, :] == jnp.arange(grid_rows, dtype=jnp.int32)[:, None, None]) & (
        slot_rank[None, None, :] == jnp.arange(capacity, dtype=jnp.int32)[None, :, None]
    )
    filled = jnp.any(picked, axis=2)
    source_index = jnp.sum(jnp.where(picked, block_iota[None, None, :], 0), axis=2)
    outgoing = jnp.where(filled[:, :, None, None], products[source_index], jnp.float32(0.0))
    incoming = lax.all_to_all(outgoing, "row", split_axis=0, concat_axis=0, tiled=True)
    return incoming.reshape(1, grid_rows * capacity, block_edge, block_edge)


def solution(mesh):
    placed = (
        P("row", "col", None, None),
        P("row", "col", None),
        P("row", "col"),
        P("row", "col", None, None),
        P("row", "col", None),
        P("row", "col"),
        P("row", "col", None),
    )
    return jax.shard_map(
        per_device,
        mesh=mesh,
        in_specs=placed,
        out_specs=P("row", "col", None, None),
        check_vma=False,
    )
```

profile of v0, /device:TPU:134, one launch (start us, length us, event | category | flops | bytes accessed | tf_op | source)
XLA Modules:
  0.0 301.8 jit_solution(11534719890570377215)
XLA Ops:
  0.0 2.1 collective-permute-start.4
  2.1 20.5 %collective-permute-start.5 = (f32[1,3,128,384]{3,2,1,0:T(8,128)}, f32[1,3,128,384]{3,2,1,0:T(8,128)S(1)}, u32[]{:S(2)}, u32[]{:S(2)}) collective-permute-start(f32[1,3,128,384]{3,2,1,0:T(8,128)} %param.10), channel_id=1, source_target_pairs={{0,960},{64,0},{128,64},{192,128},{256,192},{320,256},{384,320},{4... | collective-permute-start | bytes 1769480 | tf_op jit(solution)/shard_map/ppermute | solution.py:12
  22.5 2.3 collective-permute-start
  24.8 2.2 collective-permute-start.1
  27.0 3.3 %collective-permute-start.2 = (s32[1,3,3]{2,0,1:T(1,128)}, s32[1,3,3]{2,0,1:T(1,128)S(1)}, u32[]{:S(2)}, u32[]{:S(2)}) collective-permute-start(s32[1,3,3]{2,0,1:T(1,128)} %param.11), channel_id=1, source_target_pairs={{0,960},{64,0},{128,64},{192,128},{256,192},{320,256},{384,320},{4... | collective-permute-start | bytes 116 | tf_op jit(solution)/shard_map/ppermute | solution.py:12
  30.3 2.8 fusion.17
  33.2 0.2 convert_reduce_fusion
  33.4 0.1 fusion.32
  33.5 0.1 and_reduce_fusion
  33.6 2.3 reshape.230
  35.9 0.1 iota_compare_fusion.13
  36.0 0.1 iota_compare_fusion.12
  36.0 0.1 copy.22
  36.1 0.1 reshape.237
  36.2 0.1 copy.17
  36.3 0.7 fusion.41
  37.0 3.2 %collective-permute-start.3 = (s32[1,3]{1,0:T(1,128)S(1)}, s32[1,3]{1,0:T(1,128)S(1)}, u32[]{:S(2)}, u32[]{:S(2)}) collective-permute-start(s32[1,3]{1,0:T(1,128)S(1)} %copy-done.8), channel_id=1, source_target_pairs={{0,960},{64,0},{128,64},{192,128},{256,192},{320,256},{384,320},{4... | collective-permute-start | bytes 44 | tf_op jit(solution)/shard_map/ppermute | solution.py:12
  40.3 0.1 iota_compare_fusion.11
  40.3 9.9 %collective-permute-done.3 = s32[1,3]{1,0:T(1,128)S(1)} collective-permute-done((s32[1,3]{1,0:T(1,128)S(1)}, s32[1,3]{1,0:T(1,128)S(1)}, u32[]{:S(2)}, u32[]{:S(2)}) %collective-permute-start.3) | collective-permute-done | bytes 44 | tf_op jit(solution)/shard_map/ppermute | solution.py:12
  50.2 0.1 iota_compare_fusion.10
  50.3 25.7 %collective-permute-start.7 = (s32[1,3]{1,0:T(1,128)S(1)}, s32[1,3]{1,0:T(1,128)S(1)}, u32[]{:S(2)}, u32[]{:S(2)}) collective-permute-start(s32[1,3]{1,0:T(1,128)S(1)} %collective-permute-done.1), channel_id=1, source_target_pairs={{0,63},{1,0},{2,1},{3,2},{4,3},{5,4},{6,5},{7,6},{8,7},{9,8},{10,9... | collective-permute-start | bytes 44 | tf_op jit(solution)/shard_map/ppermute | solution.py:12
  76.0 2.7 collective-permute-done.7
  78.7 13.7 %collective-permute-start.9 = (s32[1,3]{1,0:T(1,128)S(1)}, s32[1,3]{1,0:T(1,128)S(1)}, u32[]{:S(2)}, u32[]{:S(2)}) collective-permute-start(s32[1,3]{1,0:T(1,128)S(1)} %collective-permute-done.3), channel_id=1, source_target_pairs={{0,960},{64,0},{128,64},{192,128},{256,192},{320,256},{384,320},{4... | collective-permute-start | bytes 44 | tf_op jit(solution)/shard_map/ppermute | solution.py:12
  92.4 0.1 iota_compare_fusion.9
  92.5 1.2 collective-permute-done.9
  93.7 0.1 iota_compare_fusion.8
  93.7 0.6 fusion.37
  94.4 4.4 %collective-permute-start.6 = (s32[1,3,3]{2,0,1:T(1,128)S(1)}, s32[1,3,3]{2,0,1:T(1,128)S(1)}, u32[]{:S(2)}, u32[]{:S(2)}) collective-permute-start(s32[1,3,3]{2,0,1:T(1,128)S(1)} %collective-permute-done), channel_id=1, source_target_pairs={{0,63},{1,0},{2,1},{3,2},{4,3},{5,4},{6,5},{7,6},{8,7},{9,8},{10,9... | collective-permute-start | bytes 116 | tf_op jit(solution)/shard_map/ppermute | solution.py:12
  98.8 14.7 %collective-permute-start.8 = (s32[1,3,3]{2,0,1:T(1,128)S(1)}, s32[1,3,3]{2,0,1:T(1,128)S(1)}, u32[]{:S(2)}, u32[]{:S(2)}) collective-permute-start(s32[1,3,3]{2,0,1:T(1,128)S(1)} %collective-permute-done.2), channel_id=1, source_target_pairs={{0,960},{64,0},{128,64},{192,128},{256,192},{320,256},{384,320},{4... | collective-permute-start | bytes 116 | tf_op jit(solution)/shard_map/ppermute | solution.py:12
  113.5 0.7 fusion.43
  114.2 0.6 collective-permute-done.8
  114.8 0.7 fusion.45
  115.4 0.6 fusion.39
  116.0 3.7 %collective-permute-start.10 = (f32[1,3,384,128]{3,2,1,0:T(8,128)S(1)}, f32[1,3,384,128]{3,2,1,0:T(8,128)S(1)}, u32[]{:S(2)}, u32[]{:S(2)}) collective-permute-start(f32[1,3,384,128]{3,2,1,0:T(8,128)S(1)} %collective-permute-done.4), channel_id=1, source_target_pairs={{0,63},{1,0},{2,1},{3,2},{4,3},{5,4},{6,5},{7,6},{8,7},{9,8},{10,9... | collective-permute-start | bytes 1769480 | tf_op jit(solution)/shard_map/ppermute | solution.py:12
  119.7 14.8 %collective-permute-start.11 = (f32[1,3,128,384]{3,2,1,0:T(8,128)S(1)}, f32[1,3,128,384]{3,2,1,0:T(8,128)}, u32[]{:S(2)}, u32[]{:S(2)}) collective-permute-start(f32[1,3,128,384]{3,2,1,0:T(8,128)S(1)} %collective-permute-done.5), channel_id=1, source_target_pairs={{0,960},{64,0},{128,64},{192,128},{256,192},{320,256},{384,320},{4... | collective-permute-start | bytes 1769480 | tf_op jit(solution)/shard_map/ppermute | solution.py:12
  134.5 1.5 fusion.14
  136.1 2.2 reshape.231
  138.3 9.7 %fusion.2 = f32[4,6,128,128,1,1]{3,1,5,4,2,0:T(8,128)} fusion(f32[3,3,128,3,128]{4,3,2,1,0:T(4,128)} %reshape.231, f32[3,3,6]{2,1,0:T(4,128)} %fusion.43, f32[3,3,4]{1,0,2:T(4,128)} %fusion.37), kind=kOutput, calls=%fused_computation.3 | convolution fusion | flops 127402632 | bytes 3342696 | tf_op jit(solution)/shard_map/ktiuj,ktpuq->ipjq/dot_general | solution.py:37
  148.0 31.3 %collective-permute-done.11 = f32[1,3,128,384]{3,2,1,0:T(8,128)} collective-permute-done((f32[1,3,128,384]{3,2,1,0:T(8,128)S(1)}, f32[1,3,128,384]{3,2,1,0:T(8,128)}, u32[]{:S(2)}, u32[]{:S(2)}) %collective-permute-start.11) | collective-permute-done | bytes 589856 | tf_op jit(solution)/shard_map/ppermute | solution.py:12
  179.3 2.6 fusion.11
  181.9 2.2 reshape.232
  184.2 9.0 %fusion = f32[4,6,128,128,1,1]{3,1,5,4,2,0:T(8,128)S(1)} fusion(f32[3,3,128,3,128]{4,3,2,1,0:T(4,128)} %reshape.232, f32[3,3,6]{2,1,0:T(4,128)S(1)} %copy-done.3, f32[3,3,4]{1,0,2:T(4,128)S(1)} %copy-done.1), kind=kOutput, calls=%fused_computation.1 | convolution fusion | flops 127402632 | bytes 3342696 | tf_op jit(solution)/shard_map/ktiuj,ktpuq->ipjq/dot_general | solution.py:37
  193.2 7.4 %bitcast_add_fusion = f32[4,6,128,128]{3,1,2,0:T(8,128)S(1)} fusion(f32[4,6,128,128,1,1]{3,1,5,4,2,0:T(8,128)S(1)} %fusion, f32[4,6,128,128,1,1]{3,1,5,4,2,0:T(8,128)S(1)} %copy-done.9, f32[3,3,128,3,128]{4,3,2,1,0:T(4,128)S(1)} %copy-done, f32[3,3,6]{2,1,0:T(4,128)S(1)} %copy-done.2, f32[3,3,4]{1,0,2:T(4,128)S(1)} %fusion.35), kind=kOutput, calls=%fused_computation.10 | convolution fusion | flops 128189064 | bytes 6488424 | tf_op jit(solution)/shard_map/ktiuj,ktpuq->ipjq/dot_general | solution.py:37
  200.6 0.3 copy.21
  200.8 2.0 gather_fusion
  202.8 1.8 broadcast_select_fusion
  204.6 95.8 %all_to_all.5 = f32[16,2,128,128]{3,2,1,0:T(8,128)S(1)} all-to-all(f32[16,2,128,128]{3,2,1,0:T(8,128)S(1)} %broadcast_select_fusion), channel_id=1, replica_groups=mesh['row'=16,'col'=64] {'row'}, dimensions={0} | all-to-all | bytes 4194304 | tf_op jit(solution)/shard_map/all_to_all | solution.py:65
  300.4 1.3 copy.62
  (38 shorter events, 0.1 us)
Async XLA Ops:
  0.0 33.1 %copy-start.4 = (s32[1,3,3]{2,0,1:T(1,128)S(1)}, s32[1,3,3]{2,0,1:T(1,128)}, u32[]{:S(2)}) copy-start(s32[1,3,3]{2,0,1:T(1,128)} %param.8) | copy-start | bytes 112
  0.0 33.1 %copy-start.5 = (s32[1,3,3]{2,0,1:T(1,128)S(1)}, s32[1,3,3]{2,0,1:T(1,128)}, u32[]{:S(2)}) copy-start(s32[1,3,3]{2,0,1:T(1,128)} %param.11) | copy-start | bytes 112
  0.0 33.2 %copy-start.6 = (s32[1,24,1]{1,2,0:T(1,128)S(1)}, s32[1,24,1]{1,2,0:T(1,128)}, u32[]{:S(2)}) copy-start(s32[1,24,1]{1,2,0:T(1,128)} %param.13) | copy-start | bytes 292
  0.0 116.0 %collective-permute-start.4 = (f32[1,3,384,128]{3,2,1,0:T(8,128)}, f32[1,3,384,128]{3,2,1,0:T(8,128)S(1)}, u32[]{:S(2)}, u32[]{:S(2)}) collective-permute-start(f32[1,3,384,128]{3,2,1,0:T(8,128)} %param.7), channel_id=1, source_target_pairs={{0,63},{1,0},{2,1},{3,2},{4,3},{5,4},{6,5},{7,6},{8,7},{9,8},{10,9... | collective-permute-start | bytes 1769480 | tf_op jit(solution)/shard_map/ppermute | solution.py:12
  2.1 117.6 %collective-permute-start.5 = (f32[1,3,128,384]{3,2,1,0:T(8,128)}, f32[1,3,128,384]{3,2,1,0:T(8,128)S(1)}, u32[]{:S(2)}, u32[]{:S(2)}) collective-permute-start(f32[1,3,128,384]{3,2,1,0:T(8,128)} %param.10), channel_id=1, source_target_pairs={{0,960},{64,0},{128,64},{192,128},{256,192},{320,256},{384,320},{4... | collective-permute-start | bytes 1769480 | tf_op jit(solution)/shard_map/ppermute | solution.py:12
  22.5 71.2 %collective-permute-start = (s32[1,3,3]{2,0,1:T(1,128)}, s32[1,3,3]{2,0,1:T(1,128)S(1)}, u32[]{:S(2)}, u32[]{:S(2)}) collective-permute-start(s32[1,3,3]{2,0,1:T(1,128)} %param.8), channel_id=1, source_target_pairs={{0,63},{1,0},{2,1},{3,2},{4,3},{5,4},{6,5},{7,6},{8,7},{9,8},{10,9... | collective-permute-start | bytes 116 | tf_op jit(solution)/shard_map/ppermute | solution.py:12
  24.8 12.2 %collective-permute-start.1 = (s32[1,3]{1,0:T(1,128)}, s32[1,3]{1,0:T(1,128)S(1)}, u32[]{:S(2)}, u32[]{:S(2)}) collective-permute-start(s32[1,3]{1,0:T(1,128)} %param.9), channel_id=1, source_target_pairs={{0,63},{1,0},{2,1},{3,2},{4,3},{5,4},{6,5},{7,6},{8,7},{9,8},{10,9... | collective-permute-start | bytes 44 | tf_op jit(solution)/shard_map/ppermute | solution.py:12
  27.0 71.7 %collective-permute-start.2 = (s32[1,3,3]{2,0,1:T(1,128)}, s32[1,3,3]{2,0,1:T(1,128)S(1)}, u32[]{:S(2)}, u32[]{:S(2)}) collective-permute-start(s32[1,3,3]{2,0,1:T(1,128)} %param.11), channel_id=1, source_target_pairs={{0,960},{64,0},{128,64},{192,128},{256,192},{320,256},{384,320},{4... | collective-permute-start | bytes 116 | tf_op jit(solution)/shard_map/ppermute | solution.py:12
  33.1 2.8 copy-start.7
  33.1 2.8 copy-start.8
  37.0 13.2 %collective-permute-start.3 = (s32[1,3]{1,0:T(1,128)S(1)}, s32[1,3]{1,0:T(1,128)S(1)}, u32[]{:S(2)}, u32[]{:S(2)}) collective-permute-start(s32[1,3]{1,0:T(1,128)S(1)} %copy-done.8), channel_id=1, source_target_pairs={{0,960},{64,0},{128,64},{192,128},{256,192},{320,256},{384,320},{4... | collective-permute-start | bytes 44 | tf_op jit(solution)/shard_map/ppermute | solution.py:12
  50.3 28.4 %collective-permute-start.7 = (s32[1,3]{1,0:T(1,128)S(1)}, s32[1,3]{1,0:T(1,128)S(1)}, u32[]{:S(2)}, u32[]{:S(2)}) collective-permute-start(s32[1,3]{1,0:T(1,128)S(1)} %collective-permute-done.1), channel_id=1, source_target_pairs={{0,63},{1,0},{2,1},{3,2},{4,3},{5,4},{6,5},{7,6},{8,7},{9,8},{10,9... | collective-permute-start | bytes 44 | tf_op jit(solution)/shard_map/ppermute | solution.py:12
  78.7 15.0 %collective-permute-start.9 = (s32[1,3]{1,0:T(1,128)S(1)}, s32[1,3]{1,0:T(1,128)S(1)}, u32[]{:S(2)}, u32[]{:S(2)}) collective-permute-start(s32[1,3]{1,0:T(1,128)S(1)} %collective-permute-done.3), channel_id=1, source_target_pairs={{0,960},{64,0},{128,64},{192,128},{256,192},{320,256},{384,320},{4... | collective-permute-start | bytes 44 | tf_op jit(solution)/shard_map/ppermute | solution.py:12
  94.4 19.8 %collective-permute-start.6 = (s32[1,3,3]{2,0,1:T(1,128)S(1)}, s32[1,3,3]{2,0,1:T(1,128)S(1)}, u32[]{:S(2)}, u32[]{:S(2)}) collective-permute-start(s32[1,3,3]{2,0,1:T(1,128)S(1)} %collective-permute-done), channel_id=1, source_target_pairs={{0,63},{1,0},{2,1},{3,2},{4,3},{5,4},{6,5},{7,6},{8,7},{9,8},{10,9... | collective-permute-start | bytes 116 | tf_op jit(solution)/shard_map/ppermute | solution.py:12
  98.8 16.0 %collective-permute-start.8 = (s32[1,3,3]{2,0,1:T(1,128)S(1)}, s32[1,3,3]{2,0,1:T(1,128)S(1)}, u32[]{:S(2)}, u32[]{:S(2)}) collective-permute-start(s32[1,3,3]{2,0,1:T(1,128)S(1)} %collective-permute-done.2), channel_id=1, source_target_pairs={{0,960},{64,0},{128,64},{192,128},{256,192},{320,256},{384,320},{4... | collective-permute-start | bytes 116 | tf_op jit(solution)/shard_map/ppermute | solution.py:12
  116.0 32.0 %collective-permute-start.10 = (f32[1,3,384,128]{3,2,1,0:T(8,128)S(1)}, f32[1,3,384,128]{3,2,1,0:T(8,128)S(1)}, u32[]{:S(2)}, u32[]{:S(2)}) collective-permute-start(f32[1,3,384,128]{3,2,1,0:T(8,128)S(1)} %collective-permute-done.4), channel_id=1, source_target_pairs={{0,63},{1,0},{2,1},{3,2},{4,3},{5,4},{6,5},{7,6},{8,7},{9,8},{10,9... | collective-permute-start | bytes 1769480 | tf_op jit(solution)/shard_map/ppermute | solution.py:12
  119.7 59.6 %collective-permute-start.11 = (f32[1,3,128,384]{3,2,1,0:T(8,128)S(1)}, f32[1,3,128,384]{3,2,1,0:T(8,128)}, u32[]{:S(2)}, u32[]{:S(2)}) collective-permute-start(f32[1,3,128,384]{3,2,1,0:T(8,128)S(1)} %collective-permute-done.5), channel_id=1, source_target_pairs={{0,960},{64,0},{128,64},{192,128},{256,192},{320,256},{384,320},{4... | collective-permute-start | bytes 1769480 | tf_op jit(solution)/shard_map/ppermute | solution.py:12
  181.9 2.3 copy-start.1
  181.9 2.3 copy-start.3
  184.1 9.0 %copy-start = (f32[3,3,128,3,128]{4,3,2,1,0:T(4,128)S(1)}, f32[3,3,128,3,128]{4,3,2,1,0:T(4,128)}, u32[]{:S(2)}) copy-start(f32[3,3,128,3,128]{4,3,2,1,0:T(4,128)} %reshape.230) | copy-start | bytes 5308420
  184.2 9.0 %copy-start.2 = (f32[3,3,6]{2,1,0:T(4,128)S(1)}, f32[3,3,6]{2,1,0:T(4,128)}, u32[]{:S(2)}) copy-start(f32[3,3,6]{2,1,0:T(4,128)} %fusion.41) | copy-start | bytes 652
  184.2 9.0 %copy-start.9 = (f32[4,6,128,128,1,1]{3,1,5,4,2,0:T(8,128)S(1)}, f32[4,6,128,128,1,1]{3,1,5,4,2,0:T(8,128)}, u32[]{:S(2)}) copy-start(f32[4,6,128,128,1,1]{3,1,5,4,2,0:T(8,128)} %fusion.2) | copy-start | bytes 4718596
where the time goes:
time: 302 us
  starting transfers between devices  111 us (37%)
  blocking collectives  95.8 us (32%)
  waiting for transfers between devices  45.7 us (15%)
  matrix products  32.9 us (11%)
  local copies, waits for them, and re-layouts  10.7 us (4%)
  other arithmetic  5.9 us (2%)
    ppermute x12, starting transfers between devices, passed_along(): lax.ppermute(value, axis, [(i, (i + by) % peers) for i in range(peers)])  111 us
    all_to_all x1, blocking collectives, per_device(): lax.all_to_all(outgoing, 'row', split_axis=0, concat_axis=0, tiled=True)  95.8 us
    ppermute x12, waiting for transfers between devices, passed_along(): lax.ppermute(value, axis, [(i, (i + by) % peers) for i in range(peers)])  45.7 us
    dot_general x3, matrix products, local_terms(): jnp.einsum('ktiuj,ktpuq->ipjq', pair_hot, slot_prod, precision=lax.Precis...  26 us
    dot_general x3, matrix products, local_terms(): jnp.einsum('kxb,kby->kxy', a_panel, b_panel, precision=lax.Precision.HIGH...  6.89 us
    reshape x3, local copies, waits for them, and re-layouts, local_terms(): slot_prod.reshape(inner_count, slot_count, block_edge, slot_count, block_...  6.76 us
  transfers between devices with their start and end apart: 12, of which 5 were waited for; matrix products, arithmetic and copies ran while one was open for 8% of the time, Pallas kernels for 0%

commit v1 on v0

v1 whole, which is shorter than its diff:
```python
import jax
import jax.numpy as jnp
from jax import lax
from jax.experimental import pallas as pl
from jax.experimental.pallas import tpu as pltpu
from jax.sharding import PartitionSpec as P

MESH = pl.DeviceIdType.MESH
BS = 128
SLOTS = 3
RB = 4
CB = 6
KB = 3
CAPP = 2
HALVES = 2
SIDE = 8
BLOCKS = RB * CB
CARRIERS = {0: (7, 6), 1: (4, 2)}
LANDING = {0: (0, 0), 6: (0, 2), 1: (1, 0), 4: (1, 1), 2: (1, 2)}


def kernel(a_ref, b_ref, am_ref, bm_ref, tbl_ref, out_ref,
           a_got, b_got, am_got, bm_got, carry, crossed, crossed_m,
           pah, pal, pbh, pbl, prod, stage, relay,
           a_s, a_r, b_s, b_r, c_s, c_r, x_s, x_r, f_s,
           z_s, z_r, o_s, o_r, w_s, w_r, l_s):
    row = lax.axis_index("row")
    col = lax.axis_index("col")
    n_col = lax.axis_size("col")
    half = row // SIDE
    y = lax.rem(row, SIDE)
    left = (row, lax.rem(col + n_col - 1, n_col))
    right = (row, lax.rem(col + 1, n_col))
    other = 1 - half
    across = (other * SIDE + y, col)

    def at_y(yy):
        return (half * SIDE + yy, col)

    def turned(d):
        return lax.rem(y + d, SIDE)

    def send(src, dst, ss, rs, to):
        return pltpu.make_async_remote_copy(
            src_ref=src, dst_ref=dst, send_sem=ss, recv_sem=rs, device_id=to, device_id_type=MESH)

    barrier = pltpu.get_barrier_semaphore()
    peers = [left, right, across] + [at_y(turned(d)) for d in range(1, SIDE)]
    for peer in peers:
        pl.semaphore_signal(barrier, inc=1, device_id=peer, device_id_type=MESH)
    pl.semaphore_wait(barrier, len(peers))

    def a_copy(step, k):
        if k == KB:
            src = am_ref if step == 0 else am_got.at[0]
            return send(src, am_got.at[step], a_s.at[step, k], a_r.at[step, k], left)
        src = a_ref.at[k] if step == 0 else a_got.at[0, k]
        return send(src, a_got.at[step, k], a_s.at[step, k], a_r.at[step, k], left)

    up = at_y(lax.rem(y + SIDE - 1, SIDE))

    def b_copy(step, k):
        if k == KB:
            src = bm_ref if step == 0 else bm_got.at[0]
            return send(src, bm_got.at[step], b_s.at[step, k], b_r.at[step, k], up)
        src = b_ref.at[k] if step == 0 else b_got.at[0, k]
        return send(src, b_got.at[step, k], b_s.at[step, k], b_r.at[step, k], up)

    def carry_copy(n, to):
        return send(b_ref.at[1 + n], carry, c_s.at[n], c_r.at[0], at_y(to))

    def cross_copy(src):
        return send(src, crossed, x_s.at[0], x_r.at[0], across)

    def cross_meta():
        return send(bm_ref, crossed_m, x_s.at[1], x_r.at[1], across)

    def cross_last():
        return send(carry, b_got.at[0, 1], x_s.at[0], b_r.at[0, 1], across)

    def land_copy(yy):
        panel, third = LANDING[yy]
        return send(crossed, b_got.at[panel, third], f_s.at[0], b_r.at[panel, third], at_y(SIDE - 1))

    def land_meta(yy):
        panel = LANDING[yy][0]
        return send(crossed_m, bm_got.at[panel], f_s.at[1], b_r.at[panel, KB], at_y(SIDE - 1))

    for yy, targets in CARRIERS.items():
        @pl.when(y == yy)
        def _():
            for n, to in enumerate(targets):
                carry_copy(n, to).start()
            cross_meta().start()
            cross_copy(b_ref.at[0]).start()

    @pl.when(y > 0)
    def _():
        for k in (KB, 0, 1, 2):
            b_copy(0, k).start()

    for k in (KB, 0, 1, 2):
        a_copy(0, k).start()

    def build_a(src, meta, k):
        @pl.loop(0, RB)
        def _(i):
            total = jnp.zeros((BS, BS), jnp.float32)
            for t in range(SLOTS):
                total += jnp.where(meta[pl.ds(k * SLOTS + t, 1), :] == i, src[pl.ds(t * BS, BS), :], 0.0)
            high = total.astype(jnp.bfloat16)
            rows = pl.ds(pl.multiple_of(i * BS, BS), BS)
            pah[rows, pl.ds(k * BS, BS)] = high
            pal[rows, pl.ds(k * BS, BS)] = (total - high.astype(jnp.float32)).astype(jnp.bfloat16)

    def build_b(src, meta, k):
        @pl.loop(0, CB)
        def _(j):
            total = jnp.zeros((BS, BS), jnp.float32)
            for t in range(SLOTS):
                total += jnp.where(meta[pl.ds(k * SLOTS + t, 1), :] == j, src[:, pl.ds(t * BS, BS)], 0.0)
            high = total.astype(jnp.bfloat16)
            cols = pl.ds(pl.multiple_of(j * BS, BS), BS)
            pbh[pl.ds(k * BS, BS), cols] = high
            pbl[pl.ds(k * BS, BS), cols] = (total - high.astype(jnp.float32)).astype(jnp.bfloat16)

    def multiply(first):
        @pl.loop(0, CB // 2)
        def _(pair):
            cols = pl.ds(pl.multiple_of(pair * 2 * BS, 2 * BS), 2 * BS)
            bh = pbh[:, cols]
            bl = pbl[:, cols]
            for i in range(RB // 2):
                ah = pah[pl.ds(i * 2 * BS, 2 * BS), :]
                al = pal[pl.ds(i * 2 * BS, 2 * BS), :]
                part = (jnp.dot(ah, bl, preferred_element_type=jnp.float32)
                        + jnp.dot(al, bh, preferred_element_type=jnp.float32)
                        + jnp.dot(ah, bh, preferred_element_type=jnp.float32))
                for p in range(2):
                    for q in range(2):
                        block = (i * 2 + p) * CB + pair * 2 + q
                        piece = part[p * BS:(p + 1) * BS, q * BS:(q + 1) * BS]
                        prod[block] = piece if first else prod[block] + piece

    for k in range(KB):
        build_a(a_ref.at[k], am_ref, k)
        build_b(b_ref.at[k], bm_ref, k)
    multiply(True)
    prod[BLOCKS] = jnp.zeros((BS, BS), jnp.float32)

    carriers = [to for targets in CARRIERS.values() for to in targets]
    for yy in carriers:
        @pl.when(y == yy)
        def _():
            carry_copy(0, yy).wait_recv()
            if yy == SIDE - 1:
                cross_last().start()
            else:
                cross_copy(carry).start()

    for k in (KB, 0, 1, 2):
        a_copy(0, k).wait_recv()
        a_copy(1, k).start()
    for k in (KB, 0, 1, 2):
        b_copy(0, k).wait_recv()

        @pl.when(y > 0)
        def _():
            b_copy(1, k).start()
        if k < KB:
            build_a(a_got.at[0, k], am_got.at[0], k)
            build_b(b_got.at[0, k], bm_got.at[0], k)
    multiply(False)

    for yy in LANDING:
        @pl.when(y == yy)
        def _():
            if yy in CARRIERS:
                cross_meta().wait_recv()
                land_meta(yy).start()
            cross_copy(b_ref.at[0]).wait_recv()
            land_copy(yy).start()

    for k in (KB, 0, 1, 2):
        a_copy(1, k).wait_recv()
        b_copy(1, k).wait_recv()
        if k < KB:
            build_a(a_got.at[1, k], am_got.at[1], k)
            build_b(b_got.at[1, k], bm_got.at[1], k)
    multiply(False)

    def fill(slot, owner):
        for rank in range(CAPP):
            stage[slot * CAPP + rank] = prod[tbl_ref[owner * CAPP + rank]]

    def pair_at(ref, place):
        return ref.at[pl.ds(place * CAPP, CAPP)]

    def z_copy(d):
        dst = pair_at(out_ref, row) if d == 0 else pair_at(relay, d - 1)
        return send(pair_at(stage, SIDE + d), dst, z_s.at[d], z_r.at[d], across)

    def own_copy(d):
        return send(pair_at(stage, d), pair_at(out_ref, row), o_s.at[d], o_r.at[d], at_y(turned(d)))

    def onward_copy(d):
        return send(pair_at(relay, d - 1), pair_at(out_ref, other * SIDE + y),
                    w_s.at[d], w_r.at[d], at_y(turned(d)))

    for d in (1, 2, 3, 4, 5, 6, 7, 0):
        fill(SIDE + d, other * SIDE + turned(d))
        z_copy(d).start()
        fill(d, half * SIDE + turned(d))
        if d:
            own_copy(d).start()
    kept = pltpu.make_async_copy(pair_at(stage, 0), pair_at(out_ref, row), l_s.at[0])
    kept.start()
    for d in range(1, SIDE):
        z_copy(d).wait_recv()
        onward_copy(d).start()

    for step in range(2):
        for k in range(KB + 1):
            a_copy(step, k).wait_send()

            @pl.when(y > 0)
            def _():
                b_copy(step, k).wait_send()
    for yy, targets in CARRIERS.items():
        @pl.when(y == yy)
        def _():
            for n, to in enumerate(targets):
                carry_copy(n, to).wait_send()
            cross_meta().wait_send()
            cross_copy(b_ref.at[0]).wait_send()
    for yy in carriers:
        @pl.when(y == yy)
        def _():
            cross_copy(carry).wait_send()
    for yy in LANDING:
        @pl.when(y == yy)
        def _():
            if yy in CARRIERS:
                land_meta(yy).wait_send()
            land_copy(yy).wait_send()
    kept.wait()
    for d in range(1, SIDE):
        own_copy(d).wait()
    z_copy(0).wait()
    for d in range(1, SIDE):
        z_copy(d).wait_send()
        onward_copy(d).wait()


def per_device(a_blocks, a_rowid, a_count, b_blocks, b_colid, b_count, dest_row):
    slot = jnp.arange(SLOTS, dtype=jnp.int32)

    def marks(ids, used):
        live = jnp.where(slot[None, :] < used[:, None], ids, -1).reshape(-1, 1)
        return jnp.broadcast_to(jnp.pad(live, ((0, 16 - KB * SLOTS), (0, 0))), (16, BS))

    n_row = lax.axis_size("row")
    targets = dest_row[0, :, 0]
    order = jnp.arange(BLOCKS, dtype=jnp.int32)
    earlier = (targets[:, None] == targets[None, :]) & (order[None, :] < order[:, None])
    rank = jnp.sum(earlier.astype(jnp.int32), axis=1)
    place = targets * CAPP + rank
    picked = place[None, :] == jnp.arange(n_row * CAPP, dtype=jnp.int32)[:, None]
    table = BLOCKS + jnp.sum(jnp.where(picked, order[None, :] - BLOCKS, 0), axis=1)

    vmem = pl.BlockSpec(memory_space=pltpu.VMEM)
    f32, bf16 = jnp.float32, jnp.bfloat16
    dma = pltpu.SemaphoreType.DMA
    out = pl.pallas_call(
        kernel,
        out_shape=jax.ShapeDtypeStruct((n_row * CAPP, BS, BS), f32),
        in_specs=[vmem, vmem, vmem, vmem, pl.BlockSpec(memory_space=pltpu.SMEM)],
        out_specs=pl.BlockSpec(memory_space=pl.ANY),
        scratch_shapes=[
            pltpu.VMEM((2, KB, SLOTS * BS, BS), f32),
            pltpu.VMEM((2, KB, BS, SLOTS * BS), f32),
            pltpu.VMEM((2, 16, BS), jnp.int32),
            pltpu.VMEM((2, 16, BS), jnp.int32),
            pltpu.VMEM((BS, SLOTS * BS), f32),
            pltpu.VMEM((BS, SLOTS * BS), f32),
            pltpu.VMEM((16, BS), jnp.int32),
            pltpu.VMEM((RB * BS, KB * BS), bf16),
            pltpu.VMEM((RB * BS, KB * BS), bf16),
            pltpu.VMEM((KB * BS, CB * BS), bf16),
            pltpu.VMEM((KB * BS, CB * BS), bf16),
            pltpu.VMEM((BLOCKS + 1, BS, BS), f32),
            pltpu.VMEM((HALVES * SIDE * CAPP, BS, BS), f32),
            pltpu.VMEM(((SIDE - 1) * CAPP, BS, BS), f32),
            dma((2, KB + 1)), dma((2, KB + 1)), dma((2, KB + 1)), dma((2, KB + 1)),
            dma((2,)), dma((1,)), dma((2,)), dma((2,)), dma((2,)),
            dma((SIDE,)), dma((SIDE,)), dma((SIDE,)), dma((SIDE,)),
            dma((SIDE,)), dma((SIDE,)), dma((1,)),
        ],
        compiler_params=pltpu.CompilerParams(
            collective_id=0, has_side_effects=True, vmem_limit_bytes=48 * 2**20),
        cost_estimate=pl.CostEstimate(flops=2 * 3 * 3 * 512 * 384 * 768, bytes_accessed=4 * 2**20, transcendentals=0),
        name="panels",
    )(a_blocks[0], b_blocks[0], marks(a_rowid[0], a_count[0]), marks(b_colid[0], b_count[0]), table)
    return out[None]


def solution(mesh):
    placed = (
        P("row", "col", None, None),
        P("row", "col", None),
        P("row", "col"),
        P("row", "col", None, None),
        P("row", "col", None),
        P("row", "col"),
        P("row", "col", None),
    )
    return jax.shard_map(
        per_device,
        mesh=mesh,
        in_specs=placed,
        out_specs=P("row", "col", None, None),
        check_vma=False,
    )
```

time: 302 us -> 169 us (0.56)
  the two profiles are of different devices: /device:TPU:134 before, /device:TPU:174 now
where the time goes in v1:
time: 169 us
  Pallas kernels  160 us (95%)
  other arithmetic  4.54 us (3%)
  local copies, waits for them, and re-layouts  3.96 us (2%)
    pallas_call x1, Pallas kernels, per_device(): pl.pallas_call(kernel, out_shape=jax.ShapeDtypeStruct((n_row * CAPP, BS,...  160 us
    unnamed x5, local copies, waits for them, and re-layouts  3.45 us

profile of v1, /device:TPU:174, one launch (start us, length us, event | category | flops | bytes accessed | tf_op | source)
XLA Modules:
  0.0 168.9 jit_solution(9120859871309756923)
XLA Ops:
  0.0 0.7 iota_compare_fusion.3
  0.7 0.1 lt.67
  0.8 0.7 iota_compare_fusion.2
  1.5 0.1 lt.72
  1.6 0.9 convert_reduce_fusion
  2.5 0.7 iota_add_fusion
  3.2 0.1 select_reduce_fusion
  3.3 0.7 reduce
  4.0 0.1 squeeze.17
  4.1 0.7 reduce.1
  4.8 0.1 squeeze.18
  4.9 0.1 broadcast_in_dim.45.bm_ref
  5.0 0.1 broadcast_in_dim.43.am_ref
  5.1 0.0 copy-start
  5.1 1.1 copy-done
  6.1 0.0 copy-start.1
  6.1 1.1 copy-done.1
  7.2 160.4 %panels.1 = f32[32,128,128]{2,1,0:T(8,128)S(1)} custom-call(f32[3,384,128]{2,1,0:T(8,128)S(1)} %bitcast.12, f32[3,128,384]{2,1,0:T(8,128)S(1)} %bitcast.13, s32[16,128]{1,0:T(8,128)S(1)} %broadcast_in_dim.43.am_ref, s32[16,128]{1,0:T(8,128)S(1)} %broadcast_in_dim.45.bm_ref, s32[32]{0:T(128)S(1)} %broadcast_add_fusion.tbl_ref), custom_call_target="tpu_custom_call" | custom-call | flops 2717908992 | bytes 4194304 | tf_op jit(solution)/shard_map/panels/pallas_call | solution.py:274
  167.6 1.3 copy.9
  (5 shorter events, 0.0 us)
Async XLA Ops:
  5.1 1.1 copy-start
  6.1 1.1 copy-start.1

commit v2 on v1

v2 whole, which is shorter than its diff:
```python
import jax
import jax.numpy as jnp
from jax import lax
from jax.experimental import pallas as pl
from jax.experimental.pallas import tpu as pltpu
from jax.sharding import PartitionSpec as P

MESH = pl.DeviceIdType.MESH
BS = 128
SLOTS = 3
RB = 4
CB = 6
KB = 3
CAPP = 2
LAG = 5
CHANGE = 5
WINDOW = 4
HALVES = 2
SIDE = 8
BLOCKS = RB * CB
PARTS = 4
PART = KB * BS // PARTS


def kernel(a_ref, a_id, a_used, b_ref, b_id, b_used, dest_ref, out_ref,
           am_ref, bm_ref, tbl_ref,
           a_got, b_got, am_got, bm_got, carry, crossed, crossed_m,
           pah, pal, pbh, pbl, prod, stage, relay,
           a_s, a_r, b_s, b_r, c_s, c_r, x_s, x_r, f_s,
           z_s, z_r, o_s, o_r, w_s, w_r, l_s, turn):
    row = lax.axis_index("row")
    col = lax.axis_index("col")
    n_col = lax.axis_size("col")
    half = row // SIDE
    y = lax.rem(row, SIDE)
    left = (row, lax.rem(col + n_col - 1, n_col))
    right = (row, lax.rem(col + 1, n_col))
    other = 1 - half
    across = (other * SIDE + y, col)
    inner = lax.rem(col // 2, SIDE)
    early = inner < SIDE // 2
    nearest = jnp.where(early, SIDE // 2, 2 * SIDE) - inner // 2 * 2

    def along_z(step):
        to = lax.rem(half * SIDE + inner + step, HALVES * SIDE)
        return (to // SIDE * SIDE + y, col + (lax.rem(to, SIDE) - inner) * 2)

    other_shift = [along_z(nearest + step) for step in (0, 2, SIDE, SIDE + 2)]

    first = (y == 0) | (y > PARTS)
    panel = jnp.where(first, 0, 1)
    part = jnp.where(first, lax.rem(SIDE - y, SIDE), y - 1)
    last = SIDE - 1

    def at_y(yy):
        return (half * SIDE + yy, col)

    def turned(d):
        return lax.rem(y + d, SIDE)

    def send(src, dst, ss, rs, to):
        return pltpu.make_async_remote_copy(
            src_ref=src, dst_ref=dst, send_sem=ss, recv_sem=rs, device_id=to, device_id_type=MESH)

    barrier = pltpu.get_barrier_semaphore()
    peers = [left, right, across] + other_shift + [at_y(turned(d)) for d in range(1, SIDE)]
    for peer in peers:
        pl.semaphore_signal(barrier, inc=1, device_id=peer, device_id_type=MESH)
    pl.semaphore_wait(barrier, len(peers))

    for k in range(KB):
        for t in range(SLOTS):
            a_mark = jnp.where(t < a_used[0, k], a_id[0, k, t], -1)
            b_mark = jnp.where(t < b_used[0, k], b_id[0, k, t], -1)
            am_ref[pl.ds(k * SLOTS + t, 1), :] = jnp.full((1, BS), a_mark, jnp.int32)
            bm_ref[pl.ds(k * SLOTS + t, 1), :] = jnp.full((1, BS), b_mark, jnp.int32)

    def a_copy(step, k):
        if k == KB:
            src = am_ref if step == 0 else am_got.at[0]
            return send(src, am_got.at[step], a_s.at[step, k], a_r.at[step, k], left)
        src = a_ref.at[k] if step == 0 else a_got.at[0, k]
        return send(src, a_got.at[step, k], a_s.at[step, k], a_r.at[step, k], left)

    up = at_y(lax.rem(y + SIDE - 1, SIDE))

    def rows_of(ref, n):
        return ref.at[pl.ds(pl.multiple_of(n * PART, PART), PART)]

    def b_copy(step, n):
        if n == PARTS:
            src = bm_ref if step == 0 else bm_got.at[0]
            return send(src, bm_got.at[step], b_s.at[step, n], b_r.at[step, n], up)
        src = b_ref if step == 0 else b_got.at[0]
        return send(rows_of(src, n), rows_of(b_got.at[step], n), b_s.at[step, n], b_r.at[step, n], up)

    def carry_copy(n):
        to = jnp.where(y == 0, SIDE - n, n + 1)
        return send(rows_of(b_ref, n), carry, c_s.at[n], c_r.at[0], at_y(to))

    def cross_copy(src):
        return send(src, crossed, x_s.at[0], x_r.at[0], across)

    def cross_last():
        return send(carry, rows_of(b_got.at[0], 1), x_s.at[0], b_r.at[0, 1], across)

    def cross_meta():
        return send(bm_ref, crossed_m, x_s.at[1], x_r.at[1], across)

    def land_copy():
        return send(crossed, rows_of(b_got.at[panel], part), f_s.at[0], b_r.at[panel, part], at_y(last))

    def land_meta():
        return send(crossed_m, bm_got.at[panel], f_s.at[1], b_r.at[panel, PARTS], at_y(last))

    @pl.when(y < 2)
    def _():
        cross_copy(rows_of(b_ref, 0)).start()
        cross_meta().start()
        for n in range(1, PARTS):
            carry_copy(n).start()

    @pl.when(y > 0)
    def _():
        for n in (PARTS, 0, 1, 2, 3):
            b_copy(0, n).start()

    for k in (KB, 0, 1, 2):
        a_copy(0, k).start()

    def build_a(src, meta, k):
        @pl.loop(0, RB)
        def _(i):
            total = jnp.zeros((BS, BS), jnp.float32)
            for t in range(SLOTS):
                total += jnp.where(meta[pl.ds(k * SLOTS + t, 1), :] == i, src[pl.ds(t * BS, BS), :], 0.0)
            high = total.astype(jnp.bfloat16)
            rows = pl.ds(pl.multiple_of(i * BS, BS), BS)
            pah[rows, pl.ds(k * BS, BS)] = high
            pal[rows, pl.ds(k * BS, BS)] = (total - high.astype(jnp.float32)).astype(jnp.bfloat16)

    def build_b(src, meta, k):
        @pl.loop(0, CB)
        def _(j):
            total = jnp.zeros((BS, BS), jnp.float32)
            for t in range(SLOTS):
                total += jnp.where(meta[pl.ds(k * SLOTS + t, 1), :] == j, src[pl.ds(k * BS, BS), pl.ds(t * BS, BS)], 0.0)
            high = total.astype(jnp.bfloat16)
            cols = pl.ds(pl.multiple_of(j * BS, BS), BS)
            pbh[pl.ds(k * BS, BS), cols] = high
            pbl[pl.ds(k * BS, BS), cols] = (total - high.astype(jnp.float32)).astype(jnp.bfloat16)

    def multiply(first):
        @pl.loop(0, CB // 2)
        def _(pair):
            cols = pl.ds(pl.multiple_of(pair * 2 * BS, 2 * BS), 2 * BS)
            bh = pbh[:, cols]
            bl = pbl[:, cols]
            for i in range(RB // 2):
                ah = pah[pl.ds(i * 2 * BS, 2 * BS), :]
                al = pal[pl.ds(i * 2 * BS, 2 * BS), :]
                part = (jnp.dot(ah, bl, preferred_element_type=jnp.float32)
                        + jnp.dot(al, bh, preferred_element_type=jnp.float32)
                        + jnp.dot(ah, bh, preferred_element_type=jnp.float32))
                for p in range(2):
                    for q in range(2):
                        block = (i * 2 + p) * CB + pair * 2 + q
                        piece = part[p * BS:(p + 1) * BS, q * BS:(q + 1) * BS]
                        prod[block] = piece if first else prod[block] + piece

    @pl.loop(0, HALVES * SIDE)
    def _(owner):
        first, second = BLOCKS, BLOCKS
        for m in range(BLOCKS - 1, -1, -1):
            hit = dest_ref[0, m, 0] == owner
            second = jnp.where(hit, first, second)
            first = jnp.where(hit, m, first)
        tbl_ref[owner * CAPP] = first
        tbl_ref[owner * CAPP + 1] = second

    for k in range(KB):
        build_a(a_ref.at[k], am_ref, k)
        build_b(b_ref, bm_ref, k)
    multiply(True)
    prod[BLOCKS] = jnp.zeros((BS, BS), jnp.float32)

    @pl.when((y > 1) & (y < last))
    def _():
        carry_copy(1).wait_recv()
        cross_copy(carry).start()

    @pl.when(y == last)
    def _():
        carry_copy(1).wait_recv()
        cross_last().start()

    def b_onward():
        for n in (PARTS, 0, 1, 2, 3):
            b_copy(0, n).wait_recv()

            @pl.when(y > 0)
            def _():
                b_copy(1, n).start()

    pl.when(y < last)(b_onward)
    for k in (KB, 0, 1, 2):
        a_copy(0, k).wait_recv()

    @pl.when(y < 2)
    def _():
        cross_meta().wait_recv()
        land_meta().start()

    @pl.when(y < last)
    def _():
        cross_copy(carry).wait_recv()
        land_copy().start()

    cross_copy(carry).wait_send()
    for k in (KB, 0, 1, 2):
        a_copy(1, k).start()
    pl.when(y == last)(b_onward)
    for k in range(KB):
        build_a(a_got.at[0, k], am_got.at[0], k)
        build_b(b_got.at[0], bm_got.at[0], k)
    multiply(False)

    b_copy(1, PARTS).wait_recv()
    b_copy(1, 0).wait_recv()
    for k in range(KB):
        b_copy(1, k + 1).wait_recv()
        build_b(b_got.at[1], bm_got.at[1], k)
    a_copy(1, KB).wait_recv()
    for k in range(KB):
        a_copy(1, k).wait_recv()
        build_a(a_got.at[1, k], am_got.at[1], k)
    multiply(False)

    def fill(slot, owner):
        for rank in range(CAPP):
            stage[slot * CAPP + rank] = prod[tbl_ref[owner * CAPP + rank]]

    def pair_at(ref, place):
        return ref.at[pl.ds(place * CAPP, CAPP)]

    def z_copy(d):
        dst = pair_at(out_ref, row) if d == 0 else pair_at(relay, d - 1)
        return send(pair_at(stage, SIDE + d), dst, z_s.at[d], z_r.at[d], across)

    def own_copy(d):
        return send(pair_at(stage, d), pair_at(out_ref, row), o_s.at[d], o_r.at[d], at_y(turned(d)))

    def onward_copy(d):
        return send(pair_at(relay, d - 1), pair_at(out_ref, other * SIDE + y),
                    w_s.at[d], w_r.at[d], at_y(turned(d)))

    order = (4, 3, 5, 2, 6, 1, 7, 0)
    def arrive(d):
        z_copy(d).wait_recv()
        if d == order[CHANGE]:
            @pl.when(early)
            def _():
                for peer in other_shift:
                    pl.semaphore_signal(turn, inc=1, device_id=peer, device_id_type=MESH)
        if d:
            onward_copy(d).start()

    def cross_pair(d):
        fill(SIDE + d, other * SIDE + turned(d))
        z_copy(d).start()

    def own_pairs():
        for d in range(1, SIDE):
            fill(d, half * SIDE + turned(d))
            own_copy(d).start()

    @pl.when(jnp.logical_not(early))
    def _():
        own_pairs()
        pl.semaphore_wait(turn, len(other_shift))

    for d in order[:WINDOW]:
        cross_pair(d)
    pl.when(early)(own_pairs)
    fill(0, row)
    kept = pltpu.make_async_copy(pair_at(stage, 0), pair_at(out_ref, row), l_s.at[0])
    kept.start()
    for n in range(WINDOW, SIDE):
        z_copy(order[n - WINDOW]).wait_send()
        cross_pair(order[n])
        if n >= LAG:
            arrive(order[n - LAG])
    for d in order[SIDE - LAG:]:
        arrive(d)

    for step in range(2):
        for k in range(KB + 1):
            a_copy(step, k).wait_send()

        @pl.when(y > 0)
        def _():
            for n in range(PARTS + 1):
                b_copy(step, n).wait_send()

    @pl.when(y < 2)
    def _():
        for n in range(1, PARTS):
            carry_copy(n).wait_send()
        cross_meta().wait_send()
        land_meta().wait_send()

    @pl.when(y < last)
    def _():
        land_copy().wait_send()
    kept.wait()
    for d in order[SIDE - WINDOW:]:
        z_copy(d).wait_send()
    for d in range(1, SIDE):
        own_copy(d).wait()
        onward_copy(d).wait()


def per_device(a_blocks, a_rowid, a_count, b_blocks, b_colid, b_count, dest_row):
    n_row = lax.axis_size("row")
    vmem = pl.BlockSpec(memory_space=pltpu.VMEM)
    f32, bf16 = jnp.float32, jnp.bfloat16
    smem = pl.BlockSpec(memory_space=pltpu.SMEM)
    dma = pltpu.SemaphoreType.DMA
    out = pl.pallas_call(
        kernel,
        out_shape=jax.ShapeDtypeStruct((n_row * CAPP, BS, BS), f32),
        in_specs=[vmem, smem, smem, vmem, smem, smem, smem],
        out_specs=pl.BlockSpec(memory_space=pl.ANY),
        scratch_shapes=[
            pltpu.VMEM((16, BS), jnp.int32),
            pltpu.VMEM((16, BS), jnp.int32),
            pltpu.SMEM((n_row * CAPP,), jnp.int32),
            pltpu.VMEM((2, KB, SLOTS * BS, BS), f32),
            pltpu.VMEM((2, KB * BS, SLOTS * BS), f32),
            pltpu.VMEM((2, 16, BS), jnp.int32),
            pltpu.VMEM((2, 16, BS), jnp.int32),
            pltpu.VMEM((PART, SLOTS * BS), f32),
            pltpu.VMEM((PART, SLOTS * BS), f32),
            pltpu.VMEM((16, BS), jnp.int32),
            pltpu.VMEM((RB * BS, KB * BS), bf16),
            pltpu.VMEM((RB * BS, KB * BS), bf16),
            pltpu.VMEM((KB * BS, CB * BS), bf16),
            pltpu.VMEM((KB * BS, CB * BS), bf16),
            pltpu.VMEM((BLOCKS + 1, BS, BS), f32),
            pltpu.VMEM((HALVES * SIDE * CAPP, BS, BS), f32),
            pltpu.VMEM(((SIDE - 1) * CAPP, BS, BS), f32),
            dma((2, KB + 1)), dma((2, KB + 1)), dma((2, PARTS + 1)), dma((2, PARTS + 1)),
            dma((PARTS,)), dma((1,)), dma((2,)), dma((2,)), dma((2,)),
            dma((SIDE,)), dma((SIDE,)), dma((SIDE,)), dma((SIDE,)),
            dma((SIDE,)), dma((SIDE,)), dma((1,)), pltpu.SemaphoreType.REGULAR,
        ],
        compiler_params=pltpu.CompilerParams(
            collective_id=0, has_side_effects=True, vmem_limit_bytes=48 * 2**20),
        cost_estimate=pl.CostEstimate(flops=2 * 3 * 3 * 512 * 384 * 768, bytes_accessed=4 * 2**20, transcendentals=0),
        name="panels",
    )(a_blocks[0], a_rowid, a_count, b_blocks.reshape(KB * BS, SLOTS * BS), b_colid, b_count, dest_row)
    return out[None]


def solution(mesh):
    placed = (
        P("row", "col", None, None),
        P("row", "col", None),
        P("row", "col"),
        P("row", "col", None, None),
        P("row", "col", None),
        P("row", "col"),
        P("row", "col", None),
    )
    return jax.shard_map(
        per_device,
        mesh=mesh,
        in_specs=placed,
        out_specs=P("row", "col", None, None),
        check_vma=False,
    )
```

time: 169 us -> 169 us (level)
  the two profiles are of different devices: /device:TPU:174 before, /device:TPU:337 now
where the time goes in v2:
time: 169 us
  Pallas kernels  162 us (96%)
  local copies, waits for them, and re-layouts  6.85 us (4%)
    pallas_call x1, Pallas kernels, per_device(): pl.pallas_call(kernel, out_shape=jax.ShapeDtypeStruct((n_row * CAPP, BS,...  162 us
    unnamed x12, local copies, waits for them, and re-layouts  6.85 us

profile of v2, /device:TPU:337, one launch (start us, length us, event | category | flops | bytes accessed | tf_op | source)
XLA Modules:
  0.0 169.1 jit_solution(10779028216270908993)
XLA Ops:
  0.0 0.7 copy.8.a_id
  0.7 0.7 copy.9.b_id
  1.4 0.7 copy.10.dest_ref
  2.1 0.0 copy-start
  2.1 1.1 copy-done
  3.2 0.0 copy-start.1
  3.2 1.1 copy-done.1
  4.2 0.0 copy-start.2
  4.2 0.7 copy-done.2
  4.9 0.0 copy-start.3
  4.9 0.7 copy-done.3
  5.5 162.2 %panels.1 = f32[32,128,128]{2,1,0:T(8,128)S(1)} custom-call(f32[3,384,128]{2,1,0:T(8,128)S(1)} %bitcast.4, s32[1,3,3]{2,1,0:T(4,128)S(1)} %copy.8.a_id, s32[1,3]{1,0:T(1,128)S(1)} %copy-done.2, f32[384,384]{1,0:T(8,128)S(1)} %bitcast.5, s32[1,3,3]{2,1,0:T(4,128)S(1)} %copy.9.b_id, s32[1,3]{1,0:T(1,128)S(1)} %copy-done.3, s32[1,24,1]{2,1,0:T(8,128)S(1)} %copy.10.dest_ref), custom_call_target="tpu_custom_call" | custom-call | flops 2717908992 | bytes 4194304 | tf_op jit(solution)/shard_map/panels/pallas_call | solution.py:329
  167.8 1.3 copy.12
Async XLA Ops:
  2.1 1.1 copy-start
  3.2 1.1 copy-start.1
  4.2 0.7 copy-start.2
  4.9 0.7 copy-start.3

commit v3 on v2

--- a/solution.py
+++ b/solution.py
@@ -205,6 +205,7 @@
     pl.when(y < last)(b_onward)
     for k in (KB, 0, 1, 2):
         a_copy(0, k).wait_recv()
+        a_copy(1, k).start()
 
     @pl.when(y < 2)
     def _():
@@ -217,8 +218,6 @@
         land_copy().start()
 
     cross_copy(carry).wait_send()
-    for k in (KB, 0, 1, 2):
-        a_copy(1, k).start()
     pl.when(y == last)(b_onward)
     for k in range(KB):
         build_a(a_got.at[0, k], am_got.at[0], k)

time: 169 us -> 163 us (0.964)
  the two profiles are of different devices: /device:TPU:337 before, /device:TPU:324 now
where the time goes in v3:
time: 163 us
  Pallas kernels  156 us (96%)
  local copies, waits for them, and re-layouts  6.85 us (4%)
    pallas_call x1, Pallas kernels, per_device(): pl.pallas_call(kernel, out_shape=jax.ShapeDtypeStruct((n_row * CAPP, BS,...  156 us
    unnamed x12, local copies, waits for them, and re-layouts  6.85 us

profile of v3, /device:TPU:324, one launch (start us, length us, event | category | flops | bytes accessed | tf_op | source)
XLA Modules:
  0.0 162.8 jit_solution(18075681046185846573)
XLA Ops:
  0.0 0.7 copy.8.a_id
  0.7 0.7 copy.9.b_id
  1.4 0.7 copy.10.dest_ref
  2.1 0.0 copy-start
  2.1 1.1 copy-done
  3.2 0.0 copy-start.1
  3.2 1.1 copy-done.1
  4.2 0.0 copy-start.2
  4.2 0.7 copy-done.2
  4.9 0.0 copy-start.3
  4.9 0.7 copy-done.3
  5.5 156.0 %panels.1 = f32[32,128,128]{2,1,0:T(8,128)S(1)} custom-call(f32[3,384,128]{2,1,0:T(8,128)S(1)} %bitcast.4, s32[1,3,3]{2,1,0:T(4,128)S(1)} %copy.8.a_id, s32[1,3]{1,0:T(1,128)S(1)} %copy-done.2, f32[384,384]{1,0:T(8,128)S(1)} %bitcast.5, s32[1,3,3]{2,1,0:T(4,128)S(1)} %copy.9.b_id, s32[1,3]{1,0:T(1,128)S(1)} %copy-done.3, s32[1,24,1]{2,1,0:T(8,128)S(1)} %copy.10.dest_ref), custom_call_target="tpu_custom_call" | custom-call | flops 2717908992 | bytes 4194304 | tf_op jit(solution)/shard_map/panels/pallas_call | solution.py:328
  161.5 1.3 copy.12
Async XLA Ops:
  2.1 1.1 copy-start
  3.2 1.1 copy-start.1
  4.2 0.7 copy-start.2
  4.9 0.7 copy-start.3
